TPU v7x, 32 devices: a whole 2x2x4 slice. The times are simulated.
32 devices in a mesh: blk: 8 (over y, x, core), head: 4 (over z).
Axes of the slice: x: 2, y: 2, z: 4, core: 2. Of those that a mesh axis runs over, the one named last changes fastest.
Arguments:
- tokens: bfloat16 [512, 4096], P('blk', 'head'), may hold values from -6 to 6
- queries: bfloat16 [512, 36864], P('blk', 'head'), may hold values from -600 to 600
- latents: bfloat16 [512, 576], P('blk'), may hold values from -6 to 6
- value_up: bfloat16 [64, 512, 128], P('head'), may hold values from -0.25 to 0.25
- out_proj: bfloat16 [8192, 4096], P('head', 'blk'), may hold values from -0.09375 to 0.09375
- expert_ids: int32 [512, 8], P('blk'), may hold values from 0 to 31, all different within a row; in each aligned block of 64 rows (0 to 63, 64 to 127, ...) at most 20 rows name the same one
- expert_gates: float32 [512, 8], P('blk'), may hold values from 0.05 to 0.5
- w_gate: bfloat16 [32, 4096, 2048], P('blk', None, 'head'), may hold values from -0.09375 to 0.09375
- w_up: bfloat16 [32, 4096, 2048], P('blk', None, 'head'), may hold values from -0.09375 to 0.09375
- w_down: bfloat16 [32, 2048, 4096], P('blk', None, 'head'), may hold values from -0.125 to 0.125
Outputs:
- result: bfloat16 [512, 4096], P('blk', 'head')
Inputs may be any that keep to these rules, and one draw needn't show every extreme that they name: `expert_ids`: among the tokens of one index of blk (aligned blocks of 64 rows) at most 20 choose one expert, and some expert is chosen by exactly 20 of them; the experts of one row differ.
All inputs are finite; a program needn't handle non-finite values.
Results may differ from a plain program's by a relative error of at most 0.013.
Values may be sent and summed in bfloat16 or wider, within the bound.
A program may use at most 128 MiB of HBM per device.

v0:
```python
import jax
import jax.numpy as jnp
from jax import lax
from jax.sharding import PartitionSpec as P

D = 4096
LAT = 512
ROPE = 64
QKNOPE = 128
EXPERTS = 32
CAP = 20


def per_device(
    tokens, queries, latents, value_up, out_proj, expert_ids, expert_gates, w_gate, w_up, w_down
):
    row_count = tokens.shape[0]
    heads_here = value_up.shape[0]
    first_row = lax.axis_index("blk") * row_count
    score_scale = (QKNOPE + ROPE) ** (-0.5)
    query_heads = queries.reshape(row_count, heads_here, LAT + ROPE)
    query_pos = first_row + jnp.arange(row_count, dtype=jnp.int32)
    last_query = first_row + row_count - 1
    start_state = (
        jnp.full((row_count, heads_here), -1e30, jnp.float32),
        jnp.zeros((row_count, heads_here), jnp.float32),
        jnp.zeros((row_count, heads_here, LAT), jnp.float32),
    )
    segment = lax.all_gather(latents, "blk", axis=0, tiled=True)

    def compute(state_in):
        running_max, denominator, accumulated = state_in
        key_count = segment.shape[0]
        scores = (
            jnp.einsum("qhc,kc->qhk", query_heads, segment, preferred_element_type=jnp.float32)
            * score_scale
        )
        key_pos = jnp.arange(key_count, dtype=jnp.int32)
        allowed = (key_pos[None, :] <= query_pos[:, None])[:, None, :]
        scores = jnp.where(allowed, scores, -1e30)
        new_max = jnp.maximum(running_max, jnp.max(scores, axis=2))
        exp_weights = jnp.where(allowed, jnp.exp(scores - new_max[:, :, None]), 0.0)
        denominator = jnp.sum(exp_weights, axis=2)
        accumulated = jnp.einsum(
            "qhk,kc->qhc",
            exp_weights.astype(jnp.bfloat16),
            segment[:, :LAT],
            preferred_element_type=jnp.float32,
        )
        return (new_max, denominator, accumulated)

    def keep(state_in):
        return state_in

    running_max, denominator, accumulated = lax.cond(
        jnp.int32(0) <= last_query, compute, keep, start_state
    )
    context = (accumulated / denominator[:, :, None]).astype(jnp.bfloat16)
    lifted = jnp.einsum(
        "qhc,hcv->qhv", context, value_up, preferred_element_type=jnp.float32
    ).astype(jnp.bfloat16)
    lifted = lifted.reshape(row_count, heads_here * value_up.shape[2])
    spread_out = jnp.dot(
        lax.all_gather(lifted, "blk", axis=0, tiled=True),
        out_proj,
        preferred_element_type=jnp.float32,
    )
    partial_out = lax.all_to_all(
        spread_out.astype(jnp.bfloat16), "blk", split_axis=0, concat_axis=1, tiled=True
    ).astype(spread_out.dtype)
    attended = lax.psum_scatter(
        partial_out.astype(jnp.bfloat16), "head", scatter_dimension=1, tiled=True
    ).astype(jnp.float32)
    mid_state = (tokens.astype(jnp.float32) + attended).astype(jnp.bfloat16)
    mid_wide = mid_state.astype(jnp.float32)
    squares = lax.psum(jnp.sum(mid_wide * mid_wide, axis=1), "head")
    normed = (mid_wide * lax.rsqrt(squares / D + 1e-06)[:, None]).astype(jnp.bfloat16)
    flat_ids = expert_ids.reshape(-1)
    choose_count = expert_ids.shape[1]
    onehot_ids = (flat_ids[:, None] == jnp.arange(EXPERTS, dtype=jnp.int32)[None, :]).astype(
        jnp.int32
    )
    earlier = jnp.cumsum(onehot_ids, axis=0) - onehot_ids
    ranks = jnp.sum(earlier * onehot_ids, axis=1)
    slot_ids = flat_ids * CAP + ranks
    slot_hits = jnp.arange(EXPERTS * CAP, dtype=jnp.int32)[:, None] == slot_ids[None, :]
    select = jnp.sum(
        slot_hits.astype(jnp.bfloat16).reshape(EXPERTS * CAP, row_count, choose_count), axis=2
    )
    combine = jnp.sum(
        jnp.where(slot_hits, expert_gates.reshape(-1)[None, :], 0.0).reshape(
            EXPERTS * CAP, row_count, choose_count
        ),
        axis=2,
    )
    outgoing = (
        jnp.dot(select, normed, preferred_element_type=jnp.float32)
        .astype(jnp.bfloat16)
        .reshape(EXPERTS, CAP, normed.shape[1])
    )
    incoming = lax.all_to_all(outgoing, "blk", split_axis=0, concat_axis=1, tiled=True)
    contract_segment = lax.all_gather(incoming, "head", axis=2, tiled=True)
    gate_add = jnp.einsum(
        "esd,edf->esf", contract_segment, w_gate, preferred_element_type=jnp.float32
    )
    up_add = jnp.einsum("esd,edf->esf", contract_segment, w_up, preferred_element_type=jnp.float32)
    activation = (jax.nn.silu(gate_add) * up_add).astype(jnp.bfloat16)
    expert_out = jnp.einsum(
        "esf,efd->esd",
        lax.all_gather(activation, "head", axis=2, tiled=True),
        w_down,
        preferred_element_type=jnp.float32,
    ).astype(jnp.bfloat16)
    returned = lax.all_to_all(expert_out, "blk", split_axis=1, concat_axis=0, tiled=True)
    returned_wide = returned.reshape(EXPERTS * CAP, returned.shape[2]).astype(jnp.float32)
    routed = jnp.einsum("sr,sd->rd", combine, returned_wide, precision=lax.Precision.HIGHEST)
    return (mid_wide + routed).astype(jnp.bfloat16)


def solution(mesh):
    placed = (
        P("blk", "head"),
        P("blk", "head"),
        P("blk", None),
        P("head", None, None),
        P("head", "blk"),
        P("blk", None),
        P("blk", None),
        P("blk", None, "head"),
        P("blk", None, "head"),
        P("blk", None, "head"),
    )
    return jax.shard_map(
        per_device, mesh=mesh, in_specs=placed, out_specs=P("blk", "head"), check_vma=False
    )
```

profile of v0, /device:TPU:0, one launch (start us, length us, event | category | flops | bytes accessed | tf_op | source)
XLA Modules:
  0.0 350.0 jit_solution(15849883045892427172)
XLA Ops:
  6.5 13.6 %all_gather.12 = bf16[512,576]{1,0:T(8,128)(2,1)} all-gather(bf16[64,576]{1,0:T(8,128)(2,1)} %param.14), channel_id=1, replica_groups=mesh['blk'=8,'head'=4] {'blk'}, dimensions={0}, use_global_device_ids=true | all-gather | bytes 663552 | tf_op jit(solution)/shard_map/all_gather | solution.py:29
  20.2 7.7 %conditional.1 = (f32[64,16]{1,0:T(8,128)S(1)}, f32[64,16,512]{2,1,0:T(8,128)}) conditional(s32[]{:T(128)} %convert_element_type.62, () %tuple.13, (s32[]{:T(128)}, s32[64]{0:T(128)S(1)}, bf16[64,9216]{1,0:T(8,128)(2,1)}, bf16[512,576]{1,0:T(8,128)(2,1)}) %tuple.14), branch_computations={%region_0.0_spmd, %region_1.4_spmd} | conditional | flops 1147698176 | bytes 15586096 | solution.py:55
  20.3 2.2 reshape.84
  22.5 2.3 fusion
  24.9 2.2 fusion.3
  27.0 0.9 fusion.2
  27.9 1.9 divide_convert_fusion
  30.1 1.3 fusion.19
  32.3 28.3 %all-gather.4.cloned.1.call-done = bf16[512,2048]{1,0:T(8,128)(2,1)} async-done(((bf16[64,2048]{1,0:T(8,128)(2,1)}), bf16[512,2048]{1,0:T(8,128)(2,1)}) %all-gather.4.cloned.1.call-update) | async-done | bytes 2097168 | tf_op jit(solution)/shard_map/all_gather | solution.py:64
  60.6 2.8 convolution_convert_fusion.2
  63.5 12.4 %all_to_all.52 = bf16[8,64,512]{2,1,0:T(8,128)(2,1)S(1)} all-to-all(bf16[8,64,512]{2,1,0:T(8,128)(2,1)S(1)} %bitcast.63), channel_id=1, replica_groups=mesh['blk'=8,'head'=4] {'blk'}, dimensions={0} | all-to-all | bytes 1048576 | tf_op jit(solution)/shard_map/all_to_all | solution.py:68
  75.9 0.8 copy.77
  77.1 1.2 reduce-window.6
  79.4 18.3 %reduce-scatter.2.cloned.1.call-done = bf16[64,1024]{1,0:T(8,128)(2,1)} async-done(((bf16[64,4096]{1,0:T(8,128)(2,1)}), bf16[64,1024]{1,0:T(8,128)(2,1)}) %reduce-scatter.2.cloned.1.call-update) | async-done | bytes 131088 | tf_op jit(solution)/shard_map/reduce_scatter | solution.py:71
  97.6 1.0 fusion.23
  98.7 8.7 %psum.7 = f32[64]{0:T(128)S(1)} all-reduce(f32[64]{0:T(128)S(1)} %fusion.23), channel_id=1, replica_groups=mesh['blk'=8,'head'=4] {'head'}, use_global_device_ids=true, to_apply=%region_11.12 | all-reduce | flops 64 | bytes 512 | tf_op jit(solution)/shard_map/psum | solution.py:76
  107.4 1.4 convolution_convert_fusion
  109.2 24.4 %all_to_all.53 = bf16[32,20,1024]{2,1,0:T(8,128)(2,1)S(1)} all-to-all(bf16[32,20,1024]{2,1,0:T(8,128)(2,1)S(1)} %reshape.91), channel_id=1, replica_groups=mesh['blk'=8,'head'=4] {'blk'}, dimensions={0} | all-to-all | bytes 2621440 | tf_op jit(solution)/shard_map/all_to_all | solution.py:101
  133.6 1.0 copy.70
  134.6 1.5 copy.71
  136.4 95.4 %all-gather.6.cloned.1.call-done = bf16[4,160,4096]{2,1,0:T(8,128)(2,1)} async-done(((bf16[4,160,1024]{2,1,0:T(8,128)(2,1)}), bf16[4,160,4096]{2,1,0:T(8,128)(2,1)}) %all-gather.6.cloned.1.call-update) | async-done | bytes 5242896 | tf_op jit(solution)/shard_map/all_gather | solution.py:102
  231.8 9.0 %fusion.31 = f32[4,160,512]{2,1,0:T(8,128)S(1)} fusion(bf16[4,160,4096]{2,1,0:T(8,128)(2,1)} %all-gather.6.cloned.1.call-done, bf16[4,4096,512]{2,1,0:T(8,128)(2,1)} %param.19), kind=kOutput, calls=%fused_computation.54 | convolution fusion | flops 2684354560 | bytes 23330816 | tf_op jit(solution)/shard_map/esd,edf->esf/dot_general | solution.py:103
  240.8 9.5 %fusion.17 = bf16[4,160,512]{2,1,0:T(8,128)(2,1)} fusion(bf16[4,160,4096]{2,1,0:T(8,128)(2,1)S(1)} %copy-done.2, bf16[4,4096,512]{2,1,0:T(8,128)(2,1)} %param.20, f32[4,160,512]{2,1,0:T(8,128)S(1)} %fusion.31), kind=kOutput, calls=%fused_computation.25 | convolution fusion | flops 2686320640 | bytes 23986176 | tf_op jit(solution)/shard_map/esd,edf->esf/dot_general | solution.py:106
  250.4 53.3 %all-gather.8.cloned.1.call-done = bf16[4,160,2048]{2,1,0:T(8,128)(2,1)} async-done(((bf16[4,160,512]{2,1,0:T(8,128)(2,1)}), bf16[4,160,2048]{2,1,0:T(8,128)(2,1)}) %all-gather.8.cloned.1.call-update) | async-done | bytes 2621456 | tf_op jit(solution)/shard_map/all_gather | solution.py:110
  303.7 9.4 %convolution_convert_fusion.1 = bf16[4,160,1024]{2,1,0:T(8,128)(2,1)S(1)} fusion(bf16[4,160,2048]{2,1,0:T(8,128)(2,1)} %all-gather.8.cloned.1.call-done, bf16[4,2048,1024]{2,1,0:T(8,128)(2,1)} %param.21), kind=kOutput, calls=%fused_computation.23 | convolution fusion | flops 2685009920 | bytes 20709376 | tf_op jit(solution)/shard_map/esf,efd->esd/dot_general | solution.py:108
  313.1 2.1 copy.72
  315.2 3.7 %all-to-all-start.2 = ((bf16[4,160,1024]{2,0,1:T(4,128)(2,1)}), bf16[4,160,1024]{2,0,1:T(4,128)(2,1)S(1)}, u32[]{:S(2)}, u32[]{:S(2)}) async-start(bf16[4,160,1024]{2,0,1:T(4,128)(2,1)} %copy.72), calls=%async_computation.3 | async-start | bytes 2621440 | tf_op jit(solution)/shard_map/all_to_all | solution.py:114
  319.0 1.1 select_reduce_fusion
  320.1 17.0 %all-to-all-done.2 = bf16[4,160,1024]{2,0,1:T(4,128)(2,1)S(1)} async-done(((bf16[4,160,1024]{2,0,1:T(4,128)(2,1)}), bf16[4,160,1024]{2,0,1:T(4,128)(2,1)S(1)}, u32[]{:S(2)}, u32[]{:S(2)}) %all-to-all-start.2) | async-done | bytes 1310752 | tf_op jit(solution)/shard_map/all_to_all | solution.py:114
  337.1 1.6 copy.73
  338.7 2.3 reshape.92
  341.0 2.4 fusion.20
  (45 shorter events, 3.3 us)
Async XLA Ops:
  6.5 54.1 %copy-start = (bf16[2048,512]{1,0:T(8,128)(2,1)S(1)}, bf16[2048,512]{1,0:T(8,128)(2,1)}, u32[]{:S(2)}) copy-start(bf16[2048,512]{1,0:T(8,128)(2,1)} %param.16) | copy-start | bytes 6291460
  6.5 54.1 %all-gather.4.cloned.1.call-start = ((), (), s32[]{:S(2)}) async-start(), calls=%async_computation.4 | async-start | bytes 2359296 | tf_op jit(solution)/shard_map/all_gather | solution.py:64
  22.5 2.3 copy-start.5
  27.9 2.2 copy-start.3
  32.2 65.4 %reduce-scatter.2.cloned.1.call-start = ((), (), s32[]{:S(2)}) async-start(), calls=%async_computation.5 | async-start | bytes 655360 | tf_op jit(solution)/shard_map/reduce_scatter | solution.py:71
  63.4 13.4 %copy-start.6 = (s32[64,8]{0,1:T(8,128)S(1)}, s32[64,8]{0,1:T(8,128)}, u32[]{:S(2)}) copy-start(s32[64,8]{0,1:T(8,128)} %param.17) | copy-start | bytes 6148
  63.4 34.2 %copy-start.4 = (bf16[64,1024]{1,0:T(8,128)(2,1)S(1)}, bf16[64,1024]{1,0:T(8,128)(2,1)}, u32[]{:S(2)}) copy-start(bf16[64,1024]{1,0:T(8,128)(2,1)} %param.12) | copy-start | bytes 393220
  76.7 155.1 %all-gather.6.cloned.1.call-start = ((), (), s32[]{:S(2)}) async-start(), calls=%async_computation.6 | async-start | bytes 6553600 | tf_op jit(solution)/shard_map/all_gather | solution.py:102
  136.2 167.5 %all-gather.8.cloned.1.call-start = ((), (), s32[]{:S(2)}) async-start(), calls=%async_computation.7 | async-start | bytes 3276800 | tf_op jit(solution)/shard_map/all_gather | solution.py:110
  231.8 9.0 %copy-start.2 = (bf16[4,160,4096]{2,1,0:T(8,128)(2,1)S(1)}, bf16[4,160,4096]{2,1,0:T(8,128)(2,1)}, u32[]{:S(2)}) copy-start(bf16[4,160,4096]{2,1,0:T(8,128)(2,1)} %all-gather.6.cloned.1.call-done) | copy-start | bytes 15728644
  313.1 5.7 %copy-start.7 = (f32[64,8]{0,1:T(8,128)S(1)}, f32[64,8]{0,1:T(8,128)}, u32[]{:S(2)}) copy-start(f32[64,8]{0,1:T(8,128)} %param.18) | copy-start | bytes 6148
  315.2 21.9 %all-to-all-start.2 = ((bf16[4,160,1024]{2,0,1:T(4,128)(2,1)}), bf16[4,160,1024]{2,0,1:T(4,128)(2,1)S(1)}, u32[]{:S(2)}, u32[]{:S(2)}) async-start(bf16[4,160,1024]{2,0,1:T(4,128)(2,1)} %copy.72), calls=%async_computation.3 | async-start | bytes 2621440 | tf_op jit(solution)/shard_map/all_to_all | solution.py:114
  337.1 6.3 %copy-start.1 = (bf16[2048,512]{1,0:T(8,128)(2,1)S(1)}, bf16[2048,512]{1,0:T(8,128)(2,1)}, u32[]{:S(2)}) copy-start(bf16[2048,512]{1,0:T(8,128)(2,1)} %param.16) | copy-start | bytes 6291460
Sparse Core Ops, SparseCore 0:
  32.4 28.1 all-gather.3
  76.9 20.7 reduce-scatter.1
  136.3 95.4 all-gather.5
  250.5 53.0 all-gather.7
where the time goes:
time: 350 us
  waiting for transfers between devices  212 us (61%)
  blocking collectives  59.2 us (17%)
  matrix products  40.5 us (12%)
  local copies, waits for them, and re-layouts  13.8 us (4%)
  between operations  13.3 us (4%)
  other arithmetic  6.89 us (2%)
  starting transfers between devices  3.96 us (1%)
    all_gather x1, waiting for transfers between devices, per_device(): contract_segment = lax.all_gather(incoming, 'head', axis=2, tiled=True)  95.4 us
    all_gather x1, waiting for transfers between devices, per_device(): lax.all_gather(activation, 'head', axis=2, tiled=True)  53.3 us
    all_gather x1, waiting for transfers between devices, per_device(): lax.all_gather(lifted, 'blk', axis=0, tiled=True)  28.3 us
    all_to_all x1, blocking collectives, per_device(): lax.all_to_all(outgoing, 'blk', split_axis=0, concat_axis=1, tiled=True)  24.4 us
    reduce_scatter x1, waiting for transfers between devices, per_device(): lax.psum_scatter(partial_out.astype(jnp.bfloat16), 'head', scatter_dimens...  18.3 us
    all_to_all x1, waiting for transfers between devices, per_device(): lax.all_to_all(expert_out, 'blk', split_axis=1, concat_axis=0, tiled=True)  17 us
    all_gather x1, blocking collectives, per_device(): segment = lax.all_gather(latents, 'blk', axis=0, tiled=True)  13.6 us
    all_to_all x1, blocking collectives, per_device(): lax.all_to_all(spread_out.astype(jnp.bfloat16), 'blk', split_axis=0, conc...  12.4 us
  transfers between devices with their start and end apart: 5, of which 5 were waited for; matrix products, arithmetic and copies ran while one was open for 1% of the time, Pallas kernels for 0%

commit v1 on v0

--- a/solution.py
+++ b/solution.py
@@ -1,6 +1,10 @@
+import functools
+
 import jax
 import jax.numpy as jnp
 from jax import lax
+from jax.experimental import pallas as pl
+from jax.experimental.pallas import tpu as pltpu
 from jax.sharding import PartitionSpec as P
 
 D = 4096
@@ -11,10 +15,8 @@
 CAP = 20
 
 
-def per_device(
-    tokens, queries, latents, value_up, out_proj, expert_ids, expert_gates, w_gate, w_up, w_down
-):
-    row_count = tokens.shape[0]
+def lifted_heads(queries, latents, value_up):
+    row_count = latents.shape[0]
     heads_here = value_up.shape[0]
     first_row = lax.axis_index("blk") * row_count
     score_scale = (QKNOPE + ROPE) ** (-0.5)
@@ -60,6 +62,14 @@
         "qhc,hcv->qhv", context, value_up, preferred_element_type=jnp.float32
     ).astype(jnp.bfloat16)
     lifted = lifted.reshape(row_count, heads_here * value_up.shape[2])
+    return lifted
+
+
+def by_collectives(
+    tokens, queries, latents, value_up, out_proj, expert_ids, expert_gates, w_gate, w_up, w_down
+):
+    row_count = tokens.shape[0]
+    lifted = lifted_heads(queries, latents, value_up)
     spread_out = jnp.dot(
         lax.all_gather(lifted, "blk", axis=0, tiled=True),
         out_proj,
@@ -117,6 +127,413 @@
     return (mid_wide + routed).astype(jnp.bfloat16)
 
 
+MESH = pl.DeviceIdType.MESH
+
+
+def push(src, dst, send, recv, device):
+    return pltpu.make_async_remote_copy(
+        src_ref=src, dst_ref=dst, send_sem=send, recv_sem=recv, device_id=device, device_id_type=MESH
+    )
+
+
+def greet(peers):
+    barrier = pltpu.get_barrier_semaphore()
+    for peer in peers:
+        pl.semaphore_signal(barrier, inc=1, device_id=peer, device_id_type=MESH)
+    pl.semaphore_wait(barrier, len(peers))
+
+
+def mid_kernel(
+    nb, nh, lifted_ref, piece_ref, proj_ref, mid_ref, gathered, partial, arrived, own,
+    lift_send, lift_recv, side_send, side_recv, sum_send, sum_recv,
+    z_send, z_recv, g_send, g_recv, c_send, c_recv,
+):
+    b, h = lax.axis_index("blk"), lax.axis_index("head")
+    groups = nb // 2
+    g, c = b // 2, b % 2
+    rows = lifted_ref.shape[0]
+    tall, wide = piece_ref.shape
+    sibling = (g * 2 + 1 - c, h)
+
+    def to_g(k):
+        return (g + k) % groups
+
+    def from_g(k):
+        return (g + groups - k) % groups
+
+    def to_h(k):
+        return (h + k) % nh
+
+    def from_h(k):
+        return (h + nh - k) % nh
+
+    greet(
+        [sibling]
+        + [(to_g(k) * 2 + c, h) for k in range(1, groups)]
+        + [(b, to_h(k)) for k in range(1, nh)]
+    )
+
+    def block(owner):
+        return gathered.at[pl.ds(pl.multiple_of(owner * rows, rows), rows), :]
+
+    sends = []
+
+    def launch(copy):
+        copy.start()
+        sends.append(copy)
+
+    for k in range(1, groups):
+        launch(
+            push(lifted_ref, block(b), lift_send.at[k], lift_recv.at[k], (to_g(k) * 2 + c, h))
+        )
+    launch(push(lifted_ref, block(b), side_send.at[0], side_recv.at[0], sibling))
+    gathered[pl.ds(pl.multiple_of(b * rows, rows), rows), :] = lifted_ref[...]
+
+    def attend(k):
+        group = from_g(k)
+        theirs = block(group * 2 + 1 - c)
+        push(theirs, theirs, side_send.at[k], side_recv.at[k], sibling).wait_recv()
+        both = gathered[pl.ds(pl.multiple_of(group * tall, tall), tall), :]
+        out = jnp.dot(both, proj_ref[...], preferred_element_type=jnp.float32)
+
+        @pl.when(group == h)
+        def _():
+            own[...] = out
+
+        @pl.when(group != h)
+        def _():
+            partial[group] = out.astype(jnp.bfloat16)
+            push(
+                partial.at[group], arrived.at[h], sum_send.at[group], sum_recv.at[h], (b, group)
+            ).start()
+
+    for k in range(1, groups):
+        mine = block(from_g(k) * 2 + c)
+        push(mine, mine, lift_send.at[k], lift_recv.at[k], sibling).wait_recv()
+        launch(push(mine, mine, side_send.at[k], side_recv.at[k], sibling))
+        attend(k - 1)
+    attend(groups - 1)
+
+    total = own[...] + piece_ref[...].astype(jnp.float32)
+    for k in range(1, nh):
+        theirs = arrived.at[from_h(k)]
+        push(theirs, theirs, sum_send.at[0], sum_recv.at[from_h(k)], sibling).wait_recv()
+        total = total + arrived[from_h(k)].astype(jnp.float32)
+
+    def place(head, owner):
+        return mid_ref.at[
+            pl.ds(pl.multiple_of(head * tall, tall), tall),
+            pl.ds(pl.multiple_of(owner * wide, wide), wide),
+        ]
+
+    mid_ref[
+        pl.ds(pl.multiple_of(h * tall, tall), tall), pl.ds(pl.multiple_of(b * wide, wide), wide)
+    ] = total.astype(jnp.bfloat16)
+
+    at = place(h, b)
+    for k in range(1, nh):
+        launch(push(at, at, z_send.at[k], z_recv.at[k], (b, to_h(k))))
+    for kz in range(nh):
+        at = place(from_h(kz), b)
+        if kz > 0:
+            push(at, at, z_send.at[kz], z_recv.at[kz], sibling).wait_recv()
+        for k in range(1, groups):
+            launch(push(at, at, g_send.at[kz, k], g_recv.at[kz, k], (to_g(k) * 2 + c, h)))
+        launch(push(at, at, c_send.at[kz, 0], c_recv.at[kz, 0], sibling))
+    for kz in range(nh):
+        for k in range(1, groups):
+            at = place(from_h(kz), from_g(k) * 2 + c)
+            push(at, at, g_send.at[kz, k], g_recv.at[kz, k], sibling).wait_recv()
+            launch(push(at, at, c_send.at[kz, k], c_recv.at[kz, k], sibling))
+    for kz in range(nh):
+        for k in range(groups):
+            at = place(from_h(kz), from_g(k) * 2 + 1 - c)
+            push(at, at, c_send.at[kz, k], c_recv.at[kz, k], sibling).wait_recv()
+    for copy in sends:
+        copy.wait_send()
+    for k in range(1, nh):
+        out = partial.at[to_h(k)]
+        push(out, out, sum_send.at[to_h(k)], sum_recv.at[0], sibling).wait_send()
+
+
+def mid_states(nb, nh, lifted, piece, out_proj):
+    rows, depth = lifted.shape
+    tall, wide = piece.shape
+    groups = nb // 2
+    dma = pltpu.SemaphoreType.DMA
+    vmem = pl.BlockSpec(memory_space=pltpu.VMEM)
+    return pl.pallas_call(
+        functools.partial(mid_kernel, nb, nh),
+        out_shape=jax.ShapeDtypeStruct((rows * nb, wide * nb), jnp.bfloat16),
+        in_specs=[vmem] * 3,
+        out_specs=vmem,
+        scratch_shapes=[
+            pltpu.VMEM((nb * rows, depth), jnp.bfloat16),
+            pltpu.VMEM((nh, tall, wide), jnp.bfloat16),
+            pltpu.VMEM((nh, tall, wide), jnp.bfloat16),
+            pltpu.VMEM((tall, wide), jnp.float32),
+            dma((groups,)), dma((groups,)), dma((groups,)), dma((groups,)),
+            dma((nh,)), dma((nh,)), dma((nh,)), dma((nh,)),
+            dma((nh, groups)), dma((nh, groups)), dma((nh, groups)), dma((nh, groups)),
+        ],
+        compiler_params=pltpu.CompilerParams(
+            collective_id=0, has_side_effects=True, vmem_limit_bytes=40 * 2**20
+        ),
+        cost_estimate=pl.CostEstimate(
+            flops=2 * nb * rows * depth * wide, bytes_accessed=2**23, transcendentals=0
+        ),
+        name="mid_states",
+    )(lifted, piece, out_proj)
+
+
+def expert_kernel(
+    nb, nh, mid_ref, select_ref, spread_ref, gate_ref, wg_hbm, wu_hbm, wd_hbm, out_ref,
+    wg, wu, wd, normed, picked, acts, acc, leaving, coming,
+    wg_sem, wu_sem, wd_sem, up_send, down_send, act_recv, back_send, back_recv,
+):
+    b, h = lax.axis_index("blk"), lax.axis_index("head")
+    experts, slots, count = select_ref.shape
+    hidden = wg.shape[2]
+    rows, cols = out_ref.shape
+    width = mid_ref.shape[1]
+
+    def first(e):
+        return [
+            pltpu.make_async_copy(wg_hbm.at[e], wg.at[e % 2], wg_sem.at[e % 2]),
+            pltpu.make_async_copy(wu_hbm.at[e], wu.at[e % 2], wu_sem.at[e % 2]),
+        ]
+
+    def second(e):
+        return pltpu.make_async_copy(wd_hbm.at[e], wd.at[e % 2], wd_sem.at[e % 2])
+
+    for e in range(min(2, experts)):
+        for copy in first(e):
+            copy.start()
+    for e in range(min(2, experts)):
+        second(e).start()
+
+    barrier = pltpu.get_barrier_semaphore()
+    for k in range(1, nb):
+        pl.semaphore_signal(barrier, inc=1, device_id=((b + k) % nb, h), device_id_type=MESH)
+    for k in range(1, nh):
+        pl.semaphore_signal(barrier, inc=1, device_id=(b, (h + k) % nh), device_id_type=MESH)
+
+    chunk = 32
+
+    @pl.loop(0, count // chunk)
+    def _(i):
+        at = pl.ds(pl.multiple_of(i * chunk, chunk), chunk)
+        some = mid_ref[at, :].astype(jnp.float32)
+        mean = jnp.sum(some * some, axis=1, keepdims=True) / width
+        normed[at, :] = (some * lax.rsqrt(mean + 1e-06)).astype(jnp.bfloat16)
+
+    acc[...] = jnp.zeros_like(acc)
+    pl.semaphore_wait(barrier, nb + nh - 2)
+
+    def shard(e, s):
+        return acts.at[e, s]
+
+    def up(e, s):
+        return push(shard(e, s), shard(e, s), up_send.at[e, s], act_recv.at[e, s], (b, h + 1))
+
+    def down(e, s):
+        return push(shard(e, s), shard(e, s), down_send.at[e, s], act_recv.at[e, s], (b, h - 1))
+
+    def came(e, s):
+        push(shard(e, s), shard(e, s), up_send.at[e, s], act_recv.at[e, s], ((b + 1) % nb, h)).wait_recv()
+
+    def onward(e, d):
+        @pl.when(h - d >= 0)
+        def _():
+            if d > 0:
+                came(e, h - d)
+
+            @pl.when(h + 1 < nh)
+            def _():
+                up(e, h - d).start()
+
+        @pl.when(h + d < nh)
+        def _():
+            if d > 0:
+                came(e, h + d)
+
+            @pl.when(h - 1 >= 0)
+            def _():
+                down(e, h + d).start()
+
+    def raise_up(e):
+        for copy in first(e):
+            copy.wait()
+        tile = 512
+
+        @pl.loop(0, width // tile)
+        def _(j):
+            at = pl.ds(pl.multiple_of(j * tile, tile), tile)
+            picked[:, at] = jnp.dot(
+                select_ref[e], normed[:, at], preferred_element_type=jnp.float32
+            ).astype(jnp.bfloat16)
+
+        rows_in = picked[...]
+        gate = jnp.dot(rows_in, wg[e % 2], preferred_element_type=jnp.float32)
+        more = jnp.dot(rows_in, wu[e % 2], preferred_element_type=jnp.float32)
+        acts[e, h] = (gate / (1.0 + jnp.exp(-gate)) * more).astype(jnp.bfloat16)
+        if e + 2 < experts:
+            for copy in first(e + 2):
+                copy.start()
+
+    def bring_down(e):
+        second(e).wait()
+        out = jnp.dot(acts[e, 0], wd[e % 2, 0:hidden], preferred_element_type=jnp.float32)
+        for s in range(1, nh):
+            out = out + jnp.dot(
+                acts[e, s], wd[e % 2, s * hidden : (s + 1) * hidden],
+                preferred_element_type=jnp.float32,
+            )
+        picked[:, 0:cols] = out.astype(jnp.bfloat16)
+        if e + 2 < experts:
+            second(e + 2).start()
+
+        tile = 256
+        for j in range(cols // tile):
+            at = slice(j * tile, (j + 1) * tile)
+            acc[:, at] += gate_ref[:, e : e + 1] * jnp.dot(
+                spread_ref[e], picked[:, at], preferred_element_type=jnp.float32
+            )
+
+    for t in range(experts + nh - 1):
+        if t < experts:
+            raise_up(t)
+            onward(t, 0)
+        for d in range(1, nh):
+            if 0 <= t - d < experts:
+                onward(t - d, d)
+        if 0 <= t - nh + 1 < experts:
+            bring_down(t - nh + 1)
+
+    backs = []
+    for k in range(1, nb):
+        to = (b + k) % nb
+        leaving[k] = acc[pl.ds(pl.multiple_of(to * rows, rows), rows), :].astype(jnp.bfloat16)
+        copy = push(leaving.at[k], coming.at[k], back_send.at[k], back_recv.at[k], (to, h))
+        copy.start()
+        backs.append(copy)
+    mine = pl.ds(pl.multiple_of(b * rows, rows), rows)
+    total = mid_ref[mine, pl.ds(pl.multiple_of(h * cols, cols), cols)].astype(jnp.float32)
+    total = total + acc[mine, :]
+    for k in range(1, nb):
+        backs[k - 1].wait_recv()
+        total = total + coming[k].astype(jnp.float32)
+    out_ref[...] = total.astype(jnp.bfloat16)
+    for copy in backs:
+        copy.wait_send()
+    for e in range(experts):
+        for s in range(nh):
+
+            @pl.when((h >= s) & (h + 1 < nh))
+            def _(e=e, s=s):
+                up(e, s).wait_send()
+
+            @pl.when((h <= s) & (h - 1 >= 0))
+            def _(e=e, s=s):
+                down(e, s).wait_send()
+
+
+def expert_layer(nb, nh, mid, select, spread, gates, w_gate, w_up, w_down):
+    experts, width, hidden = w_gate.shape
+    full, cols = w_down.shape[1:]
+    slots, count = select.shape[1:]
+    rows = count // nb
+    dma = pltpu.SemaphoreType.DMA
+    vmem = pl.BlockSpec(memory_space=pltpu.VMEM)
+    hbm = pl.BlockSpec(memory_space=pl.ANY)
+    return pl.pallas_call(
+        functools.partial(expert_kernel, nb, nh),
+        out_shape=jax.ShapeDtypeStruct((rows, cols), jnp.bfloat16),
+        in_specs=[vmem] * 4 + [hbm] * 3,
+        out_specs=vmem,
+        scratch_shapes=[
+            pltpu.VMEM((2, width, hidden), jnp.bfloat16),
+            pltpu.VMEM((2, width, hidden), jnp.bfloat16),
+            pltpu.VMEM((2, full, cols), jnp.bfloat16),
+            pltpu.VMEM((count, width), jnp.bfloat16),
+            pltpu.VMEM((slots, width), jnp.bfloat16),
+            pltpu.VMEM((experts, nh, slots, hidden), jnp.bfloat16),
+            pltpu.VMEM((count, cols), jnp.float32),
+            pltpu.VMEM((nb, rows, cols), jnp.bfloat16),
+            pltpu.VMEM((nb, rows, cols), jnp.bfloat16),
+            dma((2,)), dma((2,)), dma((2,)),
+            dma((experts, nh)), dma((experts, nh)), dma((experts, nh)),
+            dma((nb,)), dma((nb,)),
+        ],
+        compiler_params=pltpu.CompilerParams(
+            collective_id=1, has_side_effects=True, vmem_limit_bytes=58 * 2**20
+        ),
+        cost_estimate=pl.CostEstimate(
+            flops=6 * experts * slots * width * hidden,
+            bytes_accessed=6 * experts * width * hidden,
+            transcendentals=0,
+        ),
+        name="expert_layer",
+    )(mid, select, spread, gates, w_gate, w_up, w_down)
+
+
+def by_kernels(
+    nb, nh,
+    tokens, queries, latents, value_up, out_proj, expert_ids, expert_gates, w_gate, w_up, w_down,
+):
+    b = lax.axis_index("blk")
+    rows, cols = tokens.shape
+    ratio = nb // nh
+    part = cols // ratio
+    top = expert_ids.shape[1]
+    here = w_gate.shape[0]
+    slots = CAP * nb
+
+    routes = lax.all_gather(
+        jnp.concatenate([expert_ids.astype(jnp.float32), expert_gates], axis=1),
+        "blk", axis=0, tiled=True,
+    )
+    piece = jnp.zeros((rows * ratio, part), tokens.dtype)
+    for p in range(ratio):
+        turn = (p + b) % ratio
+        moved = lax.ppermute(
+            lax.dynamic_slice(tokens, (0, turn * part), (rows, part)),
+            ("blk", "head"),
+            [
+                (i * nh + j, (ratio * j + (p + i) % ratio) * nh + i // ratio)
+                for i in range(nb)
+                for j in range(nh)
+            ],
+        )
+        piece = lax.dynamic_update_slice(piece, moved, ((b + ratio - p) % ratio * rows, 0))
+
+    ids = routes[:, :top].astype(jnp.int32)
+    hits = ids[:, :, None] == (b * here + jnp.arange(here, dtype=jnp.int32))[None, None, :]
+    member = jnp.any(hits, axis=1)
+    gates = jnp.sum(jnp.where(hits, routes[:, top:, None], 0.0), axis=1)
+    order = jnp.arange(member.shape[0], dtype=jnp.int32)
+    rank = jnp.dot(
+        (order[:, None] > order[None, :]).astype(jnp.bfloat16),
+        member.astype(jnp.bfloat16),
+        preferred_element_type=jnp.float32,
+    ).astype(jnp.int32)
+    slot = jnp.where(member, rank, -1)
+    lanes = jnp.arange(slots, dtype=jnp.int32)
+    select = (slot.T[:, None, :] == lanes[None, :, None]).astype(jnp.bfloat16)
+    spread = (slot.T[:, :, None] == lanes[None, None, :]).astype(jnp.bfloat16)
+
+    lifted = lifted_heads(queries, latents, value_up)
+    mid = mid_states(nb, nh, lifted, piece, out_proj)
+    return expert_layer(nb, nh, mid, select, spread, gates, w_gate, w_up, w_down)
+
+
+def fitting(mesh):
+    nb, nh = mesh.shape["blk"], mesh.shape["head"]
+    if nb == 2 * nh and nb * nh <= 32:
+        return functools.partial(by_kernels, nb, nh)
+    return by_collectives
+
+
 def solution(mesh):
     placed = (
         P("blk", "head"),
@@ -131,5 +548,5 @@
         P("blk", None, "head"),
     )
     return jax.shard_map(
-        per_device, mesh=mesh, in_specs=placed, out_specs=P("blk", "head"), check_vma=False
-    )
+        fitting(mesh), mesh=mesh, in_specs=placed, out_specs=P("blk", "head"), check_vma=False
+    )

time: 350 us -> 180 us (0.51)
  waiting for transfers between devices: 212 us -> 0.01 us
  Pallas kernels: 0 us -> 125 us
  matrix products: 40.5 us -> 6.04 us
  blocking collectives: 59.2 us -> 26.4 us
  between operations: 13.3 us -> 0.12 us
    all_gather x3 -> x0, waiting for transfers between devices: 177 us -> none  [the longest x1 95.4 us: per_device(): contract_segment = lax.all_gather(incoming, 'head', axis=2, tiled=True)]
    pallas_call x0 -> x2, Pallas kernels: none -> 125 us  [the longest x1 66.2 us: expert_layer(): pl.pallas_call(functools.partial(expert_kernel, nb, nh), out_shape=jax.Sh...]
    all_to_all x2 -> x0, blocking collectives: 36.9 us -> none  [the longest x1 24.4 us: per_device(): lax.all_to_all(outgoing, 'blk', split_axis=0, concat_axis=1, tiled=True)]
    dot_general x7 -> x2, matrix products: 36 us -> 1.6 us  [the longest x1 1.38 us: lifted_heads(): jnp.einsum('qhc,hcv->qhv', context, value_up, preferred_element_type=jnp....]
    reduce_scatter x1 -> x0, waiting for transfers between devices: 18.3 us -> none  [per_device(): lax.psum_scatter(partial_out.astype(jnp.bfloat16), 'head', scatter_dimens...]
    all_to_all x1 -> x0, waiting for transfers between devices: 17 us -> none  [per_device(): lax.all_to_all(expert_out, 'blk', split_axis=1, concat_axis=0, tiled=True)]
    all_gather x1 -> x2, blocking collectives: 13.6 us -> 26.4 us  [the longest x1 15.3 us: by_kernels(): lax.all_gather(jnp.concatenate([expert_ids.astype(jnp.float32), expert_ga...]
    psum x1 -> x0, blocking collectives: 8.73 us -> none  [per_device(): squares = lax.psum(jnp.sum(mid_wide * mid_wide, axis=1), 'head')]
  transfers between devices with their start and end apart: 5 -> 2, of which waited for: 5 -> 0; matrix products, arithmetic and copies ran while one was open for 1% -> 10% of each run, Pallas kernels for 0% -> 0%
where the time goes in v1:
time: 180 us; the launch traced here: 179 us
  Pallas kernels  125 us (69%)
  blocking collectives  26.4 us (15%)
  local copies, waits for them, and re-layouts  10.9 us (6%)
  other arithmetic  7.35 us (4%)
  matrix products  6.04 us (3%)
  starting transfers between devices  2.56 us (1%)
    pallas_call x1, Pallas kernels, expert_layer(): pl.pallas_call(functools.partial(expert_kernel, nb, nh), out_shape=jax.Sh...  66.2 us
    pallas_call x1, Pallas kernels, mid_states(): pl.pallas_call(functools.partial(mid_kernel, nb, nh), out_shape=jax.Shape...  59.2 us
    all_gather x1, blocking collectives, by_kernels(): lax.all_gather(jnp.concatenate([expert_ids.astype(jnp.float32), expert_ga...  15.3 us
    all_gather x1, blocking collectives, lifted_heads(): segment = lax.all_gather(latents, 'blk', axis=0, tiled=True)  11.1 us
    unnamed x18, local copies, waits for them, and re-layouts  5.19 us
  transfers between devices with their start and end apart: 2, of which 0 were waited for; matrix products, arithmetic and copies ran while one was open for 10% of the time, Pallas kernels for 0%

profile of v1, /device:TPU:0, one launch (start us, length us, event | category | flops | bytes accessed | tf_op | source)
XLA Modules:
  0.0 178.8 jit_solution(10633622069506405961)
XLA Ops:
  0.0 1.7 constant_dynamic-slice_fusion
  1.7 2.1 %collective-permute-start = (bf16[64,512]{1,0:T(8,128)(2,1)}, bf16[64,512]{1,0:T(8,128)(2,1)}, u32[]{:S(2)}, u32[]{:S(2)}) collective-permute-start(bf16[64,512]{1,0:T(8,128)(2,1)} %get-tuple-element.29), channel_id=1, source_target_pairs={{0,0},{1,8},{2,16},{3,24},{4,4},{5,12},{6,20},{7,28},{8,1},{9,9},{... | collective-permute-start | bytes 196616 | tf_op jit(solution)/shard_map/ppermute | solution.py:499
  3.8 0.5 collective-permute-start.1
  4.2 0.7 convert_element_type.37
  4.9 0.7 maximum_bitcast_fusion
  5.6 15.3 %all-gather = f32[8,64,16]{1,2,0:T(8,128)S(1)} all-gather(f32[1,64,16]{1,2,0:T(8,128)S(1)} %maximum_bitcast_fusion), channel_id=1, replica_groups=mesh['blk'=8,'head'=4] {'blk'}, dimensions={0}, use_global_device_ids=true | all-gather | bytes 36864 | tf_op jit(solution)/shard_map/all_gather | solution.py:492
  20.9 0.1 reshape.38
  21.0 0.6 fusion.23
  21.6 0.1 compare_reduce_fusion
  21.7 0.2 fusion.20
  21.9 1.4 fusion.17.spread_ref
  23.3 1.1 fusion.18.select_ref
  24.3 11.1 %all_gather.6 = bf16[512,576]{1,0:T(8,128)(2,1)} all-gather(bf16[64,576]{1,0:T(8,128)(2,1)S(1)} %copy-done.5), channel_id=1, replica_groups=mesh['blk'=8,'head'=4] {'blk'}, dimensions={0}, use_global_device_ids=true | all-gather | bytes 663552 | tf_op jit(solution)/shard_map/all_gather | solution.py:31
  35.4 7.7 %conditional.1 = (f32[64,16]{1,0:T(8,128)S(1)}, f32[64,16,512]{2,1,0:T(8,128)}) conditional(s32[]{:T(128)} %convert_element_type.33, () %tuple.13, (s32[]{:T(128)}, s32[64]{0:T(128)S(1)}, bf16[64,9216]{1,0:T(8,128)(2,1)}, bf16[512,576]{1,0:T(8,128)(2,1)}) %tuple.14), branch_computations={%region_0.1_spmd, %region_1.4_spmd} | conditional | flops 1147698176 | bytes 15586096 | solution.py:57
  35.4 0.1 iota_compare_fusion
  35.5 2.2 %reshape.34 = bf16[64,16,576]{2,1,0:T(8,128)(2,1)S(1)} reshape(bf16[64,9216]{1,0:T(8,128)(2,1)} %get-tuple-element.25) | data formatting | bytes 2359296 | tf_op jit(solution)/shard_map/reshape | solution.py:23
  37.8 2.3 %fusion = (f32[64,16]{1,0:T(8,128)S(1)}, f32[64,16,512]{2,1,0:T(8,128)S(1)}) fusion(pred[64,512]{1,0:T(8,128)(4,1)S(1)} %iota_compare_fusion, bf16[64,16,576]{2,1,0:T(8,128)(2,1)S(1)} %reshape.34, bf16[512,576]{1,0:T(8,128)(2,1)} %get-tuple-element.19), kind=kOutput, calls=%fused_computation.2 | convolution fusion | flops 605551616 | bytes 3903488 | tf_op jit(solution)/shard_map/cond/branch_1_fun/qhc,kc->qhk/dot_general | solution.py:37
  40.1 2.1 %fusion.3 = f32[64,16,512]{2,1,0:T(8,128)} fusion(f32[64,16,512]{2,1,0:T(8,128)S(1)} %get-tuple-element.27, f32[64,16]{1,0:T(8,128)S(1)} %broadcast_maximum_fusion, pred[64,512]{1,0:T(8,128)(4,1)S(1)} %iota_compare_fusion, bf16[512,576]{1,0:T(8,128)(2,1)S(1)} %copy-done.4), kind=kOutput, calls=%fused_computation.5 | convolution fusion | flops 539492352 | bytes 4784128 | tf_op jit(solution)/shard_map/cond/branch_1_fun/qhk,kc->qhc/dot_general | solution.py:46
  42.2 0.9 fusion.2
  43.1 1.8 %divide_convert_fusion = bf16[64,16,512]{2,1,0:T(8,128)(2,1)S(1)} fusion(f32[64,16,512]{2,1,0:T(8,128)} %get-tuple-element.22, f32[64,16]{1,0:T(8,128)S(1)} %get-tuple-element.23), kind=kLoop, calls=%fused_computation.22 | loop fusion | flops 1048576 | bytes 3149824 | tf_op jit(solution)/shard_map/convert_element_type | solution.py:60
  45.0 1.4 fusion.19
  46.3 0.1 copy.38
  46.4 0.1 fusion.22
  46.5 0.9 copy.31.gate_ref
  47.4 0.0 collective-permute-done
  47.4 0.9 constant_dynamic-update-slice_fusion.1
  48.3 0.0 copy-start.3
  48.3 1.6 copy-done.3
  49.9 59.2 %mid_states.1.mid_ref = bf16[512,4096]{1,0:T(8,128)(2,1)S(1)} custom-call(bf16[64,2048]{1,0:T(8,128)(2,1)S(1)} %bitcast.23, bf16[128,512]{1,0:T(8,128)(2,1)S(1)} %constant_dynamic-update-slice_fusion.piece_ref, bf16[2048,512]{1,0:T(8,128)(2,1)S(1)} %copy-done.3), custom_call_target="tpu_custom_call" | custom-call | flops 1073741824 | bytes 8388608 | tf_op jit(solution)/shard_map/mid_states/pallas_call | solution.py:265
  109.1 1.9 %copy-done.2 = bf16[512,4096]{1,0:T(8,128)(2,1)} copy-done((bf16[512,4096]{1,0:T(8,128)(2,1)}, bf16[512,4096]{1,0:T(8,128)(2,1)S(1)}, u32[]{:S(2)}) %copy-start.2) | copy-done | bytes 4194328
  111.0 66.2 %expert_layer.1 = bf16[64,1024]{1,0:T(8,128)(2,1)} custom-call(bf16[512,4096]{1,0:T(8,128)(2,1)} %copy-done.2, bf16[4,160,512]{2,1,0:T(8,128)(2,1)} %fusion.18.select_ref, bf16[4,512,160]{2,1,0:T(8,128)(2,1)} %fusion.17.spread_ref, f32[512,4]{1,0:T(8,128)} %copy.31.gate_ref, bf16[4,4096,512]{2,1,0:T(8,128)(2,1)} %wg_hbm.1, bf16[4,4096,512]{2,1,0:T(8,128)(2,1)} %wu_hbm.1, ...), custom_call_target="tpu_custom_call" | custom-call | flops 8053063680 | bytes 50331648 | tf_op jit(solution)/shard_map/expert_layer/pallas_call | solution.py:449
  177.2 1.6 copy.46
  (23 shorter events, 0.1 us)
Async XLA Ops:
  0.0 44.9 %copy-start = (bf16[16,512,128]{2,1,0:T(8,128)(2,1)S(1)}, bf16[16,512,128]{2,1,0:T(8,128)(2,1)}, u32[]{:S(2)}) copy-start(bf16[16,512,128]{2,1,0:T(8,128)(2,1)} %param.15) | copy-start | bytes 6291460
  0.0 24.3 %copy-start.5 = (bf16[64,576]{1,0:T(8,128)(2,1)S(1)}, bf16[64,576]{1,0:T(8,128)(2,1)}, u32[]{:S(2)}) copy-start(bf16[64,576]{1,0:T(8,128)(2,1)} %param.14) | copy-start | bytes 221188
  1.7 45.7 %collective-permute-start = (bf16[64,512]{1,0:T(8,128)(2,1)}, bf16[64,512]{1,0:T(8,128)(2,1)}, u32[]{:S(2)}, u32[]{:S(2)}) collective-permute-start(bf16[64,512]{1,0:T(8,128)(2,1)} %get-tuple-element.29), channel_id=1, source_target_pairs={{0,0},{1,8},{2,16},{3,24},{4,4},{5,12},{6,20},{7,28},{8,1},{9,9},{... | collective-permute-start | bytes 196616 | tf_op jit(solution)/shard_map/ppermute | solution.py:499
  3.8 44.5 %collective-permute-start.1 = (bf16[64,512]{1,0:T(8,128)(2,1)}, bf16[64,512]{1,0:T(8,128)(2,1)S(1)}, u32[]{:S(2)}, u32[]{:S(2)}) collective-permute-start(bf16[64,512]{1,0:T(8,128)(2,1)} %get-tuple-element.28), channel_id=1, source_target_pairs={{0,4},{1,12},{2,20},{3,28},{4,0},{5,8},{6,16},{7,24},{8,5},{9,13},... | collective-permute-start | bytes 196616 | tf_op jit(solution)/shard_map/ppermute | solution.py:499
  4.2 17.3 %copy-start.7 = (s32[4]{0:T(128)}, s32[4]{0:T(128)S(1)}, u32[]{:S(2)}) copy-start(s32[4]{0:T(128)S(1)} %iota_add_fusion) | copy-start | bytes 52
  37.8 2.3 %copy-start.4 = (bf16[512,576]{1,0:T(8,128)(2,1)S(1)}, bf16[512,576]{1,0:T(8,128)(2,1)}, u32[]{:S(2)}) copy-start(bf16[512,576]{1,0:T(8,128)(2,1)} %get-tuple-element.19) | copy-start | bytes 1769476 | tf_op jit(solution)/shard_map/cond
  44.9 1.5 copy-start.6
  44.9 1.5 copy-start.8
  48.3 1.6 copy-start.3
  109.1 1.9 %copy-start.2 = (bf16[512,4096]{1,0:T(8,128)(2,1)}, bf16[512,4096]{1,0:T(8,128)(2,1)S(1)}, u32[]{:S(2)}) copy-start(bf16[512,4096]{1,0:T(8,128)(2,1)S(1)} %mid_states.1.mid_ref) | copy-start | bytes 12582916
  111.0 67.8 %copy-start.1 = (bf16[16,512,128]{2,1,0:T(8,128)(2,1)S(1)}, bf16[16,512,128]{2,1,0:T(8,128)(2,1)}, u32[]{:S(2)}) copy-start(bf16[16,512,128]{2,1,0:T(8,128)(2,1)} %param.15) | copy-start | bytes 6291460
